TPU v7x, 32 devices: a whole 2x2x4 slice. The times are simulated.
32 devices in a mesh: dp: 2 (over core), ctx: 2 (over y), feat: 8 (over z, x).
Axes of the slice: x: 2, y: 2, z: 4, core: 2. Of those that a mesh axis runs over, the one named last changes fastest.
Arguments:
- out_grads: bfloat16 [512, 28672], P(('dp', 'ctx'), 'feat'), may hold values from -6 to 6
- acts: bfloat16 [512, 8192], P(('dp', 'ctx'), 'feat'), may hold values from -6 to 6
- domain_ids: int32 [512], P(('dp', 'ctx')), may hold values from 0 to 7
- domain_weights: int32 [8], replicated, may hold values from 1 to 4
Outputs:
- grad_factor: bfloat16 [28672, 28672], P(('dp', 'ctx'), 'feat')
- act_factor: bfloat16 [8192, 8192], P(('dp', 'ctx'), 'feat')
All inputs are finite; a program needn't handle non-finite values.
Results may differ from a plain program's by a relative error of at most 0.003.
Values may be sent and summed in bfloat16 or wider, within the bound.
A program may use at most 128 MiB of HBM per device.

v0:
```python
import jax
import jax.numpy as jnp
from jax import lax
from jax.sharding import PartitionSpec as P


def from_root(block, axis, owner):
    block = jnp.where(lax.axis_index(axis) == owner, block, jnp.zeros_like(block))
    return lax.psum(block, axis)


def weigh_rows(tok_ids, rows, domain_weights):
    labels = jnp.arange(domain_weights.shape[0], dtype=jnp.int32)
    match = tok_ids[:, None] == labels[None, :]
    tok_weight = jnp.sum(jnp.where(match, domain_weights[None, :], 0), axis=1).astype(jnp.float32)
    return (tok_weight[:, None] * rows.astype(jnp.float32)).astype(jnp.bfloat16)


def contract_tokens(left, right):
    return lax.dot_general(
        left, right, (((0,), (0,)), ((), ())), preferred_element_type=jnp.float32
    )


def local(out_grads, acts, domain_ids, domain_weights):
    group_size = lax.axis_size(("dp", "ctx"))
    inv_count = 1.0 / (out_grads.shape[0] * group_size)
    all_grads, all_acts, all_ids = (
        lax.all_gather(out_grads, ("dp", "ctx"), axis=0, tiled=True),
        lax.all_gather(acts, ("dp", "ctx"), axis=0, tiled=True),
        lax.all_gather(domain_ids, ("dp", "ctx"), axis=0, tiled=True),
    )
    tile_ratio = lax.axis_size("feat") // group_size
    first_root = lax.axis_index(("dp", "ctx")) * tile_ratio
    grad_tiles = []
    act_tiles = []
    for portion in range(tile_ratio):
        copy_grads, copy_acts = (
            from_root(all_grads, "feat", first_root + portion),
            from_root(all_acts, "feat", first_root + portion),
        )
        grad_tiles.append(copy_grads)
        act_tiles.append(copy_acts)
    col_grads = jnp.concatenate(grad_tiles, axis=1)
    col_acts = jnp.concatenate(act_tiles, axis=1)
    grad_sum = contract_tokens(col_grads, weigh_rows(all_ids, all_grads, domain_weights))
    act_sum = contract_tokens(col_acts, weigh_rows(all_ids, all_acts, domain_weights))
    grad_factor = (grad_sum * inv_count).astype(jnp.bfloat16)
    act_factor = (act_sum * inv_count).astype(jnp.bfloat16)
    return (grad_factor, act_factor)


def solution(mesh):
    in_specs = (P(("dp", "ctx"), "feat"), P(("dp", "ctx"), "feat"), P(("dp", "ctx")), P())
    out_specs = (P(("dp", "ctx"), "feat"), P(("dp", "ctx"), "feat"))
    return jax.shard_map(local, mesh=mesh, in_specs=in_specs, out_specs=out_specs, check_vma=False)
```

profile of v0, /device:TPU:5, one launch (start us, length us, event | category | flops | bytes accessed | tf_op | source)
XLA Modules:
  0.0 412.8 jit_solution(9581914616323882101)
XLA Ops:
  7.2 0.0 all-gather.6.cloned.1.call-start
  7.2 0.7 all-gather.6.cloned.1.call-update
  7.9 0.0 all-gather.4.cloned.1.call-start
  7.9 0.7 all-gather.4.cloned.1.call-update
  8.6 0.0 all-reduce.3.cloned.1.call-start
  8.7 18.1 %all-gather.6.cloned.1.call-done = bf16[512,1024]{1,0:T(8,128)(2,1)} async-done(((bf16[128,1024]{1,0:T(8,128)(2,1)}), bf16[512,1024]{1,0:T(8,128)(2,1)}) %all-gather.6.cloned.1.call-update) | async-done | bytes 1048592 | tf_op jit(solution)/shard_map/all_gather | solution.py:30
  26.8 2.7 broadcast_select_fusion.3
  29.5 30.4 %all-gather.4.cloned.1.call-done = bf16[512,3584]{1,0:T(8,128)(2,1)} async-done(((bf16[128,3584]{1,0:T(8,128)(2,1)}), bf16[512,3584]{1,0:T(8,128)(2,1)}) %all-gather.4.cloned.1.call-update) | async-done | bytes 3670032 | tf_op jit(solution)/shard_map/all_gather | solution.py:29
  59.9 5.6 %broadcast_select_fusion.1 = (bf16[512,3584]{1,0:T(8,128)(2,1)}, bf16[512,3584]{1,0:T(8,128)(2,1)}) fusion(bf16[512,3584]{1,0:T(8,128)(2,1)} %all-gather.4.cloned.1.call-done, pred[]{:T(512)S(6)} %eq.10, pred[]{:T(512)S(6)} %eq.11), kind=kLoop, calls=%fused_computation.8 | loop fusion | flops 3670016 | bytes 11010050 | tf_op jit(solution)/shard_map/jit(_where)/select_n | solution.py:8
  65.4 0.0 copy-start.1
  65.4 0.0 copy-start.2
  65.4 0.0 all-reduce.3.cloned.1.call-update
  65.5 0.6 copy-done.1
  66.1 6.1 %all-gather = s32[4,1,128]{2,1,0:T(1,128)S(1)} all-gather(s32[1,1,128]{2,1,0:T(1,128)S(1)} %bitcast.3), channel_id=1, replica_groups=mesh['dp'=2,'ctx'=2,'feat'=8] {'dp','ctx'}, dimensions={0}, use_global_device_ids=true | all-gather | bytes 2560 | tf_op jit(solution)/shard_map/all_gather | solution.py:31
  72.2 0.0 copy-done.2
  72.2 0.1 select_reduce_fusion
  72.3 294.3 %all-reduce.3.cloned.1.call-done = (bf16[512,3584]{1,0:T(8,128)(2,1)}, bf16[512,3584]{1,0:T(8,128)(2,1)}, bf16[512,1024]{1,0:T(8,128)(2,1)}, bf16[512,1024]{1,0:T(8,128)(2,1)}) async-done(((bf16[512,3584]{1,0:T(8,128)(2,1)}, bf16[512,3584]{1,0:T(8,128)(2,1)}, bf16[512,1024]{1,0:T(8,128)(2,1)}, bf16[512,1024]{1,0:T(8,128)(2,1)}), (bf16[512,3584]{1,0:T(8,128)(2,1)}, bf16[512,3584]{1,0:T(8,128)(2,1)}, ...) | async-done | bytes 9437200 | tf_op jit(solution)/shard_map/psum | solution.py:9
  366.6 0.0 copy-start
  366.6 0.0 copy-start.3
  366.6 35.1 %multiply_convert_fusion = bf16[7168,3584]{1,0:T(8,128)(2,1)} fusion(bf16[512,3584]{1,0:T(8,128)(2,1)} %get-tuple-element.2, bf16[512,3584]{1,0:T(8,128)(2,1)} %get-tuple-element.3, bf16[512,3584]{1,0:T(8,128)(2,1)} %all-gather.4.cloned.1.call-done, f32[512]{0:T(512)S(1)} %convert_element_type.26), kind=kOutput, calls=%fused_computation | convolution fusion | flops 26378240000 | bytes 62392320 | tf_op jit(solution)/shard_map/dot_general | solution.py:20
  401.7 0.0 copy-done
  401.7 0.0 copy-done.3
  401.7 0.0 copy-done.4
  401.7 4.5 %multiply_convert_fusion.1 = bf16[2048,1024]{1,0:T(8,128)(2,1)} fusion(bf16[512,1024]{1,0:T(8,128)(2,1)S(1)} %copy-done.3, bf16[512,1024]{1,0:T(8,128)(2,1)S(1)} %copy-done.4, bf16[512,1024]{1,0:T(8,128)(2,1)S(1)} %copy-done, f32[512]{0:T(512)S(1)} %convert_element_type.26), kind=kOutput, calls=%fused_computation.1 | convolution fusion | flops 2157445120 | bytes 7342080 | tf_op jit(solution)/shard_map/dot_general | solution.py:20
  (2 shorter events, 0.0 us)
Async XLA Ops:
  7.2 19.6 %all-gather.6.cloned.1.call-start = ((), (), s32[]{:S(2)}) async-start(), calls=%async_computation.1 | async-start | bytes 1310720 | tf_op jit(solution)/shard_map/all_gather | solution.py:30
  7.9 52.0 %all-gather.4.cloned.1.call-start = ((), (), s32[]{:S(2)}) async-start(), calls=%async_computation | async-start | bytes 4587520 | tf_op jit(solution)/shard_map/all_gather | solution.py:29
  8.6 357.9 %all-reduce.3.cloned.1.call-start = ((), (), s32[]{:S(2)}) async-start(), calls=%async_computation.2 | async-start | bytes 18874368 | tf_op jit(solution)/shard_map/psum | solution.py:9
  65.4 0.7 copy-start.1
  65.4 6.8 %copy-start.2 = (s32[8]{0:T(128)S(1)}, s32[8]{0:T(128)}, u32[]{:S(2)}) copy-start(s32[8]{0:T(128)} %param.7) | copy-start | bytes 100
  366.6 35.2 %copy-start = (bf16[512,1024]{1,0:T(8,128)(2,1)S(1)}, bf16[512,1024]{1,0:T(8,128)(2,1)}, u32[]{:S(2)}) copy-start(bf16[512,1024]{1,0:T(8,128)(2,1)} %all-gather.6.cloned.1.call-done) | copy-start | bytes 3145732
  366.6 35.2 %copy-start.3 = (bf16[512,1024]{1,0:T(8,128)(2,1)S(1)}, bf16[512,1024]{1,0:T(8,128)(2,1)}, u32[]{:S(2)}) copy-start(bf16[512,1024]{1,0:T(8,128)(2,1)} %get-tuple-element.4) | copy-start | bytes 3145732
  366.6 35.2 %copy-start.4 = (bf16[512,1024]{1,0:T(8,128)(2,1)S(1)}, bf16[512,1024]{1,0:T(8,128)(2,1)}, u32[]{:S(2)}) copy-start(bf16[512,1024]{1,0:T(8,128)(2,1)} %get-tuple-element.5) | copy-start | bytes 3145732
Sparse Core Ops, SparseCore 0:
  9.6 17.1 all-gather.5
  28.3 31.5 all-gather.3
  65.6 300.9 all-reduce.2
where the time goes:
time: 414 us; the launch traced here: 413 us
  waiting for transfers between devices  344 us (83%)
  matrix products  39.6 us (10%)
  between operations  13.8 us (3%)
  other arithmetic  8.34 us (2%)
  blocking collectives  6.1 us (1%)
    psum x1, waiting for transfers between devices, from_root(): return lax.psum(block, axis)  294 us
    dot_general x2, matrix products, contract_tokens(): lax.dot_general(left, right, (((0,), (0,)), ((), ())), preferred_element_...  39.6 us
    all_gather x1, waiting for transfers between devices, local(): lax.all_gather(out_grads, ('dp', 'ctx'), axis=0, tiled=True)  30.4 us
    all_gather x1, waiting for transfers between devices, local(): lax.all_gather(acts, ('dp', 'ctx'), axis=0, tiled=True)  18.1 us
  transfers between devices with their start and end apart: 3, of which 3 were waited for; matrix products, arithmetic and copies ran while one was open for 1% of the time, Pallas kernels for 0%

commit v1 on v0

v1 whole, which is shorter than its diff:
```python
import functools

import jax
import jax.numpy as jnp
from jax import lax
from jax.experimental import pallas as pl
from jax.experimental.pallas import tpu as pltpu
from jax.sharding import PartitionSpec as P

MESH = pl.DeviceIdType.MESH
LANES = 128
ROW_STEP = 32
VMEM_LIMIT = 56 * 1024 * 1024


def gather_kernel(sizes, width, mine_ref, cols_ref, rows_ref,
                  own_sem, fill_sem, swap_send, swap_recv, down_send, up_send, flow_recv,
                  side_send, side_recv):
    n_dp, n_ctx, n_feat = sizes
    group = n_dp * n_ctx
    ratio = n_feat // group
    tokens = mine_ref.shape[0]
    pieces = tokens // ROW_STEP
    steps = group * pieces

    dp, ctx, feat = lax.axis_index("dp"), lax.axis_index("ctx"), lax.axis_index("feat")
    me = dp * n_ctx + ctx
    stage, lane = feat // ratio, feat % ratio

    def in_group(other):
        return {"dp": other // n_ctx, "ctx": other % n_ctx, "feat": feat}

    def on_feat(other):
        return {"dp": dp, "ctx": ctx, "feat": other}

    mates = [lax.rem(me + shift, group) for shift in range(1, group)]
    sides = [stage * ratio + lax.rem(lane + shift, ratio) for shift in range(1, ratio)]
    has_down, has_up = stage > 0, stage < group - 1

    barrier = pltpu.get_barrier_semaphore()
    for mate in mates:
        pl.semaphore_signal(barrier, inc=1, device_id=in_group(mate), device_id_type=MESH)
    for side in sides:
        pl.semaphore_signal(barrier, inc=1, device_id=on_feat(side), device_id_type=MESH)

    @pl.when(has_down)
    def _():
        pl.semaphore_signal(barrier, inc=1, device_id=on_feat(feat - ratio), device_id_type=MESH)

    @pl.when(has_up)
    def _():
        pl.semaphore_signal(barrier, inc=1, device_id=on_feat(feat + ratio), device_id_type=MESH)

    near = has_down.astype(jnp.int32) + has_up.astype(jnp.int32)
    pl.semaphore_wait(barrier, len(mates) + len(sides) + near)

    my_rows = cols_ref.at[pl.ds(pl.multiple_of(me * tokens, tokens), tokens)]
    own = pltpu.make_async_copy(mine_ref, my_rows, own_sem)
    own.start()

    def swap(shift):
        return pltpu.make_async_remote_copy(
            src_ref=mine_ref, dst_ref=my_rows,
            send_sem=swap_send.at[shift], recv_sem=swap_recv.at[group - shift],
            device_id=in_group(lax.rem(me + shift, group)), device_id_type=MESH)

    def swapped(shift):
        block = lax.rem(me + shift, group)
        rows = cols_ref.at[pl.ds(pl.multiple_of(block * tokens, tokens), tokens)]
        return pltpu.make_async_remote_copy(
            src_ref=mine_ref, dst_ref=rows,
            send_sem=swap_send.at[shift], recv_sem=swap_recv.at[shift],
            device_id=in_group(block), device_id_type=MESH)

    half = group // 2
    order = [(k % 2) * half + k // 2 for k in range(group)] if group % 2 == 0 else list(range(group))
    for shift in order[1:]:
        swap(shift).start()
    own.wait()

    is_root = stage == me
    is_flow = jnp.logical_not(is_root)
    send_down = jnp.logical_and(stage <= me, has_down)
    send_up = jnp.logical_and(stage >= me, has_up)

    def block_of(k):
        shift = (k % 2) * half + k // 2 if group % 2 == 0 else k
        return shift, lax.rem(me + shift, group)

    def span(q):
        shift, block = block_of(q // pieces)
        start = block * tokens + (q % pieces) * ROW_STEP
        return pl.ds(pl.multiple_of(start, ROW_STEP), ROW_STEP)

    def from_root(q):
        return cols_ref.at[span(q), pl.ds(0, width)]

    def landed(q, which):
        return rows_ref.at[which, span(q)]

    def remote(src, q, which, send, recv, target):
        return pltpu.make_async_remote_copy(
            src_ref=src, dst_ref=landed(q, which), send_sem=send, recv_sem=recv,
            device_id=on_feat(target), device_id_type=MESH)

    def fill(k):
        _, block = block_of(k)
        rows = pl.ds(pl.multiple_of(block * tokens, tokens), tokens)
        return pltpu.make_async_copy(
            cols_ref.at[rows, pl.ds(0, width)], rows_ref.at[lane, rows], fill_sem.at[k])

    def send_on(src, q):
        @pl.when(send_down)
        def _():
            remote(src, q, lane, down_send.at[q], flow_recv.at[q], feat - ratio).start()

        @pl.when(send_up)
        def _():
            remote(src, q, lane, up_send.at[q], flow_recv.at[q], feat + ratio).start()

        for i, side in enumerate(sides):
            remote(src, q, lane, side_send.at[i, q], side_recv.at[ratio - 2 - i, q], side).start()

    @pl.when(is_root)
    def _():
        def body(q, carry):
            k = q // pieces

            @pl.when(jnp.logical_and(q % pieces == 0, k > 0))
            def _():
                shift, _ = block_of(k)
                swapped(shift).wait_recv()

            @pl.when(q % pieces == 0)
            def _():
                fill(k).start()

            send_on(from_root(q), q)
            return carry

        lax.fori_loop(0, steps, body, 0)

        def settle(k, carry):
            fill(k).wait()
            return carry

        lax.fori_loop(0, group, settle, 0)

    @pl.when(is_flow)
    def _():
        def body(q, carry):
            remote(landed(q, lane), q, lane, down_send.at[q], flow_recv.at[q], feat).wait_recv()
            send_on(landed(q, lane), q)
            return carry

        lax.fori_loop(0, steps, body, 0)
        for shift in order[1:]:
            swapped(shift).wait_recv()

    def drain(q, carry):
        here = landed(q, lane)
        for i in range(ratio - 1):
            other = lax.rem(lane + i + 1, ratio)
            remote(here, q, other, side_send.at[i, q], side_recv.at[i, q], feat).wait_recv()
            remote(here, q, lane, side_send.at[i, q], side_recv.at[i, q], feat).wait_send()

        @pl.when(send_down)
        def _():
            remote(here, q, lane, down_send.at[q], flow_recv.at[q], feat).wait_send()

        @pl.when(send_up)
        def _():
            remote(here, q, lane, up_send.at[q], flow_recv.at[q], feat).wait_send()

        return carry

    lax.fori_loop(0, steps, drain, 0)
    for shift in order[1:]:
        swap(shift).wait_send()


def gather_tiles(mine, sizes, width):
    n_dp, n_ctx, n_feat = sizes
    group = n_dp * n_ctx
    ratio = n_feat // group
    tokens = mine.shape[0]
    steps = group * (tokens // ROW_STEP)
    dma = pltpu.SemaphoreType.DMA
    return pl.pallas_call(
        functools.partial(gather_kernel, sizes, width),
        out_shape=(
            jax.ShapeDtypeStruct((group * tokens, mine.shape[1]), mine.dtype),
            jax.ShapeDtypeStruct((ratio, group * tokens, width), mine.dtype),
        ),
        in_specs=[pl.BlockSpec(memory_space=pl.ANY)],
        out_specs=(pl.BlockSpec(memory_space=pl.ANY), pl.BlockSpec(memory_space=pl.ANY)),
        scratch_shapes=[
            dma, dma((group,)), dma((group,)), dma((group,)),
            dma((steps,)), dma((steps,)), dma((steps,)),
            dma((max(ratio - 1, 1), steps)), dma((max(ratio - 1, 1), steps)),
        ],
        compiler_params=pltpu.CompilerParams(
            collective_id=0, has_side_effects=True, vmem_limit_bytes=VMEM_LIMIT),
        name="gather_tiles",
    )(mine)


def gram_kernel(grad_steps, wide, inv_count, cols_ref, rows_ref, grad_ref, act_ref, weighted, turned):
    step = pl.program_id(0)
    both = weighted.shape[1]
    tile = grad_ref.shape[0]

    @pl.when(step == 0)
    def _():
        slab = 64

        def weigh(i, carry):
            at = pl.ds(pl.multiple_of(i * slab, slab), slab)
            scale = cols_ref[at, pl.ds(both, LANES)].astype(jnp.float32)[:, :1]
            weighted[at, :] = (cols_ref[at, pl.ds(0, both)].astype(jnp.float32) * scale).astype(jnp.bfloat16)
            return carry

        lax.fori_loop(0, weighted.shape[0] // slab, weigh, 0)

    turned[...] = rows_ref[0].T

    def tiles(out_ref, offset):
        chunk = tile if out_ref.shape[1] % tile == 0 else LANES
        for n in range(out_ref.shape[1] // chunk):
            total = jnp.dot(turned[...], weighted[:, pl.ds(offset + n * chunk, chunk)],
                            preferred_element_type=jnp.float32)
            out_ref[:, pl.ds(n * chunk, chunk)] = (total * inv_count).astype(jnp.bfloat16)

    @pl.when(step < grad_steps)
    def _():
        tiles(grad_ref, 0)

    @pl.when(step >= grad_steps)
    def _():
        tiles(act_ref, wide)


def gram(cols, rows, wide, narrow, inv_count):
    ratio, tokens, both = rows.shape
    tile = next(t for t in (512, 256, 128) if wide % t == 0 and narrow % t == 0)
    grad_tiles, act_tiles = wide // tile, narrow // tile
    grad_steps, act_steps = ratio * grad_tiles, ratio * act_tiles

    def row_block(i):
        j = jnp.maximum(i - grad_steps, 0)
        late = i >= grad_steps
        return (jnp.where(late, j // act_tiles, i // grad_tiles), 0,
                jnp.where(late, grad_tiles + j % act_tiles, i % grad_tiles))

    return pl.pallas_call(
        functools.partial(gram_kernel, grad_steps, wide, inv_count),
        grid=(grad_steps + act_steps,),
        out_shape=(
            jax.ShapeDtypeStruct((ratio * wide, wide), jnp.bfloat16),
            jax.ShapeDtypeStruct((ratio * narrow, narrow), jnp.bfloat16),
        ),
        in_specs=[
            pl.BlockSpec(cols.shape, lambda i: (0, 0)),
            pl.BlockSpec((1, tokens, tile), row_block),
        ],
        out_specs=(
            pl.BlockSpec((tile, wide), lambda i: (jnp.minimum(i, grad_steps - 1), 0)),
            pl.BlockSpec((tile, narrow), lambda i: (jnp.maximum(i - grad_steps, 0), 0)),
        ),
        scratch_shapes=[
            pltpu.VMEM((tokens, both), jnp.bfloat16),
            pltpu.VMEM((tile, tokens), jnp.bfloat16),
        ],
        compiler_params=pltpu.CompilerParams(vmem_limit_bytes=VMEM_LIMIT),
        cost_estimate=pl.CostEstimate(
            flops=2 * tokens * ratio * (wide * wide + narrow * narrow),
            bytes_accessed=2 * (ratio * (wide * wide + narrow * narrow) + rows.size + cols.size),
            transcendentals=0),
        name="gram",
    )(cols, rows)


def local(sizes, out_grads, acts, domain_ids, domain_weights):
    tokens, wide = out_grads.shape
    narrow = acts.shape[1]
    inv_count = 1.0 / (tokens * sizes[0] * sizes[1])
    labels = jnp.arange(domain_weights.shape[0], dtype=jnp.int32)
    match = domain_ids[:, None] == labels[None, :]
    weight = jnp.sum(jnp.where(match, domain_weights[None, :], 0), axis=1).astype(jnp.bfloat16)
    mine = jnp.concatenate(
        [out_grads, acts, jnp.broadcast_to(weight[:, None], (tokens, LANES))], axis=1)
    cols, rows = gather_tiles(mine, sizes, wide + narrow)
    return gram(cols, rows, wide, narrow, inv_count)


def solution(mesh):
    sizes = tuple(mesh.shape[name] for name in ("dp", "ctx", "feat"))
    in_specs = (P(("dp", "ctx"), "feat"), P(("dp", "ctx"), "feat"), P(("dp", "ctx")), P())
    out_specs = (P(("dp", "ctx"), "feat"), P(("dp", "ctx"), "feat"))
    return jax.shard_map(
        functools.partial(local, sizes), mesh=mesh, in_specs=in_specs, out_specs=out_specs, check_vma=False)
```

time: 414 us -> 233 us (0.56)
  the two profiles are of different devices: /device:TPU:5 before, /device:TPU:0 now
where the time goes in v1:
time: 233 us
  Pallas kernels  229 us (98%)
  other arithmetic  3.14 us (1%)
    pallas_call x1, Pallas kernels, gather_tiles(): pl.pallas_call(functools.partial(gather_kernel, sizes, width), out_shape=...  186 us
    pallas_call x1, Pallas kernels, gram(): pl.pallas_call(functools.partial(gram_kernel, grad_steps, wide, inv_count...  43.2 us

profile of v1, /device:TPU:0, one launch (start us, length us, event | category | flops | bytes accessed | tf_op | source)
XLA Modules:
  0.0 232.9 jit_solution(2229158595609114001)
XLA Ops:
  0.6 0.8 select_reduce_fusion
  1.4 0.1 broadcast_in_dim.23
  1.5 2.4 %pad_maximum_fusion.mine_ref = bf16[128,4736]{1,0:T(8,128)(2,1)} fusion(bf16[128,128]{1,0:T(8,128)(2,1)S(1)} %broadcast_in_dim.23, bf16[128,1024]{1,0:T(8,128)(2,1)} %param.5, bf16[128,3584]{1,0:T(8,128)(2,1)} %param.4), kind=kLoop, calls=%fused_computation | loop fusion | flops 3637248 | bytes 2424832 | tf_op jit(solution)/shard_map/concatenate | solution.py:290
  3.9 185.9 %gather_tiles.1 = (bf16[512,4736]{1,0:T(8,128)(2,1)}, bf16[2,512,4608]{2,1,0:T(8,128)(2,1)}) custom-call(bf16[128,4736]{1,0:T(8,128)(2,1)} %pad_maximum_fusion.mine_ref), custom_call_target="tpu_custom_call" | custom-call | tf_op jit(solution)/shard_map/gather_tiles/pallas_call | solution.py:189
  189.7 43.2 %gram.1 = (bf16[7168,3584]{1,0:T(8,128)(2,1)}, bf16[2048,1024]{1,0:T(8,128)(2,1)}) custom-call(bf16[512,4736]{1,0:T(8,128)(2,1)} %get-tuple-element.4.cols_ref, bf16[2,512,4608]{2,1,0:T(8,128)(2,1)} %get-tuple-element.5.rows_ref), custom_call_target="tpu_custom_call" | custom-call | flops 28454158336 | bytes 69861376 | tf_op jit(solution)/shard_map/gram/pallas_call | solution.py:255
  (1 shorter events, 0.0 us)

commit v2 on v1

v2 whole, which is shorter than its diff:
```python
import functools

import jax
import jax.numpy as jnp
from jax import lax
from jax.experimental import pallas as pl
from jax.experimental.pallas import tpu as pltpu
from jax.sharding import PartitionSpec as P

MESH = pl.DeviceIdType.MESH
LANES = 128
VMEM_LIMIT = 56 * 1024 * 1024


def gather_kernel(sizes, pieces, grads_ref, acts_ref, scale_ref, weighted_ref, turned_ref,
                  cols_ref, rows_ref, swap_send, swap_recv, down_send, up_send, flow_recv,
                  side_send, side_recv):
    n_dp, n_ctx, n_feat = sizes
    group = n_dp * n_ctx
    ratio = n_feat // group
    tokens, wide = grads_ref.shape
    width = wide + acts_ref.shape[1]
    row_step, col_step = tokens // pieces, width // pieces
    steps = group * pieces

    dp, ctx, feat = lax.axis_index("dp"), lax.axis_index("ctx"), lax.axis_index("feat")
    me = dp * n_ctx + ctx
    stage, lane = feat // ratio, feat % ratio

    def in_group(other):
        return {"dp": other // n_ctx, "ctx": other % n_ctx, "feat": feat}

    def on_feat(other):
        return {"dp": dp, "ctx": ctx, "feat": other}

    mates = [lax.rem(me + shift, group) for shift in range(1, group)]
    sides = [stage * ratio + lax.rem(lane + shift, ratio) for shift in range(1, ratio)]
    has_down, has_up = stage > 0, stage < group - 1

    my_start = pl.multiple_of(me * tokens, tokens)
    my_rows = cols_ref.at[pl.ds(my_start, tokens)]
    cols_ref[pl.ds(my_start, tokens), pl.ds(0, wide)] = grads_ref[...]
    cols_ref[pl.ds(my_start, tokens), pl.ds(wide, width - wide)] = acts_ref[...]
    cols_ref[pl.ds(my_start, tokens), pl.ds(width, LANES)] = scale_ref[...]

    barrier = pltpu.get_barrier_semaphore()
    for mate in mates:
        pl.semaphore_signal(barrier, inc=1, device_id=in_group(mate), device_id_type=MESH)
    for side in sides:
        pl.semaphore_signal(barrier, inc=1, device_id=on_feat(side), device_id_type=MESH)

    @pl.when(has_down)
    def _():
        pl.semaphore_signal(barrier, inc=1, device_id=on_feat(feat - ratio), device_id_type=MESH)

    @pl.when(has_up)
    def _():
        pl.semaphore_signal(barrier, inc=1, device_id=on_feat(feat + ratio), device_id_type=MESH)

    near = has_down.astype(jnp.int32) + has_up.astype(jnp.int32)
    pl.semaphore_wait(barrier, len(mates) + len(sides) + near)

    def swap(shift):
        return pltpu.make_async_remote_copy(
            src_ref=my_rows, dst_ref=my_rows,
            send_sem=swap_send.at[shift], recv_sem=swap_recv.at[group - shift],
            device_id=in_group(lax.rem(me + shift, group)), device_id_type=MESH)

    def swapped(shift):
        block = lax.rem(me + shift, group)
        rows = cols_ref.at[pl.ds(pl.multiple_of(block * tokens, tokens), tokens)]
        return pltpu.make_async_remote_copy(
            src_ref=my_rows, dst_ref=rows,
            send_sem=swap_send.at[shift], recv_sem=swap_recv.at[shift],
            device_id=in_group(block), device_id_type=MESH)

    half = group // 2
    order = [(k % 2) * half + k // 2 for k in range(group)] if group % 2 == 0 else list(range(group))
    for shift in order[1:]:
        swap(shift).start()

    is_root = stage == me
    is_flow = jnp.logical_not(is_root)
    send_down = jnp.logical_and(stage <= me, has_down)
    send_up = jnp.logical_and(stage >= me, has_up)

    def block_of(k):
        shift = (k % 2) * half + k // 2 if group % 2 == 0 else k
        return shift, lax.rem(me + shift, group)

    def span(q):
        shift, block = block_of(q // pieces)
        start = block * tokens + (q % pieces) * row_step
        return pl.ds(pl.multiple_of(start, row_step), row_step)

    def from_root(q):
        return cols_ref.at[span(q), pl.ds(0, width)]

    def landed(q, which):
        return rows_ref.at[which, span(q)]

    def remote(src, q, which, send, recv, target):
        return pltpu.make_async_remote_copy(
            src_ref=src, dst_ref=landed(q, which), send_sem=send, recv_sem=recv,
            device_id=on_feat(target), device_id_type=MESH)

    def send_on(src, q):
        @pl.when(send_down)
        def _():
            remote(src, q, lane, down_send.at[q], flow_recv.at[q], feat - ratio).start()

        @pl.when(send_up)
        def _():
            remote(src, q, lane, up_send.at[q], flow_recv.at[q], feat + ratio).start()

        for i, side in enumerate(sides):
            remote(src, q, lane, side_send.at[i, q], side_recv.at[ratio - 2 - i, q], side).start()

    def turn(src_ref, which, block, part):
        at = pl.ds(pl.multiple_of(block * tokens, tokens), tokens)
        start = pl.multiple_of(part * col_step, LANES)
        if src_ref is cols_ref:
            piece = src_ref[at, pl.ds(start, col_step)]
        else:
            piece = src_ref[which, at, pl.ds(start, col_step)]
        out = pl.ds(pl.multiple_of(which * width + start, LANES), col_step)
        turned_ref[out, at] = piece.T

    def finish(k, part):
        shift, block = block_of(k)

        @pl.when(jnp.logical_and(is_flow, jnp.logical_and(part == 0, k > 0)))
        def _():
            swapped(shift).wait_recv()

        at = pl.ds(pl.multiple_of(block * tokens + part * row_step, row_step), row_step)
        scale = cols_ref[at, pl.ds(width, LANES)].astype(jnp.float32)[:, :1]
        weighted_ref[at, :] = (cols_ref[at, pl.ds(0, width)].astype(jnp.float32) * scale).astype(jnp.bfloat16)

        @pl.when(is_root)
        def _():
            turn(cols_ref, lane, block, part)

        @pl.when(is_flow)
        def _():
            turn(rows_ref, lane, block, part)

        for i in range(ratio - 1):
            other = lax.rem(lane + i + 1, ratio)

            @pl.when(part == 0)
            def _():
                def arrive(j, carry):
                    q = k * pieces + j
                    remote(landed(q, other), q, other, side_send.at[i, q], side_recv.at[i, q], feat).wait_recv()
                    return carry

                lax.fori_loop(0, pieces, arrive, 0)

            turn(rows_ref, other, block, part)

    def body(q, carry):
        k, part = q // pieces, q % pieces

        @pl.when(is_root)
        def _():
            @pl.when(jnp.logical_and(part == 0, k > 0))
            def _():
                shift, _ = block_of(k)
                swapped(shift).wait_recv()

            send_on(from_root(q), q)

        @pl.when(is_flow)
        def _():
            remote(landed(q, lane), q, lane, down_send.at[q], flow_recv.at[q], feat).wait_recv()
            send_on(landed(q, lane), q)

        @pl.when(k > 0)
        def _():
            finish(k - 1, part)

        return carry

    lax.fori_loop(0, steps, body, 0)

    def last(part, carry):
        finish(group - 1, part)
        return carry

    lax.fori_loop(0, pieces, last, 0)

    def drain(q, carry):
        here = landed(q, lane)
        for i in range(ratio - 1):
            remote(here, q, lane, side_send.at[i, q], side_recv.at[i, q], feat).wait_send()

        @pl.when(send_down)
        def _():
            remote(here, q, lane, down_send.at[q], flow_recv.at[q], feat).wait_send()

        @pl.when(send_up)
        def _():
            remote(here, q, lane, up_send.at[q], flow_recv.at[q], feat).wait_send()

        return carry

    lax.fori_loop(0, steps, drain, 0)
    for shift in order[1:]:
        swap(shift).wait_send()


def gather_tiles(grads, acts, scale, sizes):
    n_dp, n_ctx, n_feat = sizes
    group = n_dp * n_ctx
    ratio = n_feat // group
    tokens, wide = grads.shape
    width = wide + acts.shape[1]
    pieces = next(p for p in (4, 2, 1) if width % (p * LANES) == 0)
    steps = group * pieces
    dma = pltpu.SemaphoreType.DMA
    vmem = pl.BlockSpec(memory_space=pltpu.VMEM)
    return pl.pallas_call(
        functools.partial(gather_kernel, sizes, pieces),
        out_shape=(
            jax.ShapeDtypeStruct((group * tokens, width), grads.dtype),
            jax.ShapeDtypeStruct((ratio * width, group * tokens), grads.dtype),
        ),
        in_specs=[vmem] * 3,
        out_specs=(vmem, vmem),
        scratch_shapes=[
            pltpu.VMEM((group * tokens, width + LANES), grads.dtype),
            pltpu.VMEM((ratio, group * tokens, width), grads.dtype),
            dma((group,)), dma((group,)),
            dma((steps,)), dma((steps,)), dma((steps,)),
            dma((max(ratio - 1, 1), steps)), dma((max(ratio - 1, 1), steps)),
        ],
        compiler_params=pltpu.CompilerParams(
            collective_id=0, has_side_effects=True, vmem_limit_bytes=VMEM_LIMIT),
        name="gather_tiles",
    )(grads, acts, scale)


def gram_kernel(grad_steps, wide, inv_count, weighted_ref, turned_ref, grad_ref, act_ref):
    step = pl.program_id(0)
    tile = grad_ref.shape[0]

    def tiles(out_ref, offset):
        chunk = tile if out_ref.shape[1] % tile == 0 else LANES
        for n in range(out_ref.shape[1] // chunk):
            total = jnp.dot(turned_ref[...], weighted_ref[:, pl.ds(offset + n * chunk, chunk)],
                            preferred_element_type=jnp.float32)
            out_ref[:, pl.ds(n * chunk, chunk)] = (total * inv_count).astype(jnp.bfloat16)

    @pl.when(step < grad_steps)
    def _():
        tiles(grad_ref, 0)

    @pl.when(step >= grad_steps)
    def _():
        tiles(act_ref, wide)


def gram(weighted, turned, wide, narrow, inv_count):
    tokens, both = weighted.shape
    ratio = turned.shape[0] // both
    tile = next(t for t in (512, 256, 128) if wide % t == 0 and narrow % t == 0)
    grad_tiles, act_tiles = wide // tile, narrow // tile
    grad_steps, act_steps = ratio * grad_tiles, ratio * act_tiles
    lane_tiles = grad_tiles + act_tiles

    def row_block(i):
        j = jnp.maximum(i - grad_steps, 0)
        late = i >= grad_steps
        return (jnp.where(late, (j // act_tiles) * lane_tiles + grad_tiles + j % act_tiles,
                          (i // grad_tiles) * lane_tiles + i % grad_tiles), 0)

    return pl.pallas_call(
        functools.partial(gram_kernel, grad_steps, wide, inv_count),
        grid=(grad_steps + act_steps,),
        out_shape=(
            jax.ShapeDtypeStruct((ratio * wide, wide), jnp.bfloat16),
            jax.ShapeDtypeStruct((ratio * narrow, narrow), jnp.bfloat16),
        ),
        in_specs=[
            pl.BlockSpec((tokens, both), lambda i: (0, 0)),
            pl.BlockSpec((tile, tokens), row_block),
        ],
        out_specs=(
            pl.BlockSpec((tile, wide), lambda i: (jnp.minimum(i, grad_steps - 1), 0)),
            pl.BlockSpec((tile, narrow), lambda i: (jnp.maximum(i - grad_steps, 0), 0)),
        ),
        compiler_params=pltpu.CompilerParams(vmem_limit_bytes=VMEM_LIMIT),
        cost_estimate=pl.CostEstimate(
            flops=2 * tokens * ratio * (wide * wide + narrow * narrow),
            bytes_accessed=2 * (ratio * (wide * wide + narrow * narrow) + turned.size + weighted.size),
            transcendentals=0),
        name="gram",
    )(weighted, turned)


def local(sizes, out_grads, acts, domain_ids, domain_weights):
    tokens, wide = out_grads.shape
    narrow = acts.shape[1]
    inv_count = 1.0 / (tokens * sizes[0] * sizes[1])
    labels = jnp.arange(domain_weights.shape[0], dtype=jnp.int32)
    match = domain_ids[:, None] == labels[None, :]
    weight = jnp.sum(jnp.where(match, domain_weights[None, :], 0), axis=1).astype(jnp.bfloat16)
    scale = jnp.broadcast_to(weight[:, None], (tokens, LANES))
    weighted, turned = gather_tiles(out_grads, acts, scale, sizes)
    return gram(weighted, turned, wide, narrow, inv_count)


def solution(mesh):
    sizes = tuple(mesh.shape[name] for name in ("dp", "ctx", "feat"))
    in_specs = (P(("dp", "ctx"), "feat"), P(("dp", "ctx"), "feat"), P(("dp", "ctx")), P())
    out_specs = (P(("dp", "ctx"), "feat"), P(("dp", "ctx"), "feat"))
    return jax.shard_map(
        functools.partial(local, sizes), mesh=mesh, in_specs=in_specs, out_specs=out_specs, check_vma=False)
```

time: 233 us -> 165 us (0.71)
  the two profiles are of different devices: /device:TPU:0 before, /device:TPU:5 now
where the time goes in v2:
time: 165 us
  Pallas kernels  163 us (99%)
    pallas_call x1, Pallas kernels, gather_tiles(): pl.pallas_call(functools.partial(gather_kernel, sizes, pieces), out_shape...  124 us
    pallas_call x1, Pallas kernels, gram(): pl.pallas_call(functools.partial(gram_kernel, grad_steps, wide, inv_count...  38.7 us

profile of v2, /device:TPU:5, one launch (start us, length us, event | category | flops | bytes accessed | tf_op | source)
XLA Modules:
  0.0 165.0 jit_solution(9785270308460701345)
XLA Ops:
  0.6 0.8 select_reduce_fusion
  1.4 0.7 broadcast_in_dim.23.scale_ref
  2.1 124.2 %gather_tiles.1 = (bf16[512,4608]{1,0:T(8,128)(2,1)}, bf16[9216,512]{1,0:T(8,128)(2,1)}) custom-call(bf16[128,3584]{1,0:T(8,128)(2,1)} %grads_ref.1, bf16[128,1024]{1,0:T(8,128)(2,1)} %acts_ref.1, bf16[128,128]{1,0:T(8,128)(2,1)} %broadcast_in_dim.23.scale_ref), custom_call_target="tpu_custom_call" | custom-call | tf_op jit(solution)/shard_map/gather_tiles/pallas_call | solution.py:223
  126.3 38.7 %gram.1 = (bf16[7168,3584]{1,0:T(8,128)(2,1)}, bf16[2048,1024]{1,0:T(8,128)(2,1)}) custom-call(bf16[512,4608]{1,0:T(8,128)(2,1)} %get-tuple-element.4.weighted_ref, bf16[9216,512]{1,0:T(8,128)(2,1)} %get-tuple-element.5.turned_ref), custom_call_target="tpu_custom_call" | custom-call | flops 28454158336 | bytes 69730304 | tf_op jit(solution)/shard_map/gram/pallas_call | solution.py:278
  (1 shorter events, 0.0 us)

commit v3 on v2

--- a/solution.py
+++ b/solution.py
@@ -9,18 +9,19 @@
 
 MESH = pl.DeviceIdType.MESH
 LANES = 128
+LAG = 2
 VMEM_LIMIT = 56 * 1024 * 1024
 
 
-def gather_kernel(sizes, pieces, grads_ref, acts_ref, scale_ref, weighted_ref, turned_ref,
-                  cols_ref, rows_ref, swap_send, swap_recv, down_send, up_send, flow_recv,
+def gather_kernel(sizes, pieces, grads_ref, acts_ref, scale_ref, weighted_out, turned_out,
+                  cols_ref, rows_ref, weighted_ref, turned_ref, weighted_sem, turned_sem, swap_send, swap_recv, down_send, up_send, flow_recv,
                   side_send, side_recv):
     n_dp, n_ctx, n_feat = sizes
     group = n_dp * n_ctx
     ratio = n_feat // group
     tokens, wide = grads_ref.shape
     width = wide + acts_ref.shape[1]
-    row_step, col_step = tokens // pieces, width // pieces
+    col_step = width // pieces
     steps = group * pieces
 
     dp, ctx, feat = lax.axis_index("dp"), lax.axis_index("ctx"), lax.axis_index("feat")
@@ -89,15 +90,17 @@
         return shift, lax.rem(me + shift, group)
 
     def span(q):
-        shift, block = block_of(q // pieces)
-        start = block * tokens + (q % pieces) * row_step
-        return pl.ds(pl.multiple_of(start, row_step), row_step)
+        _, block = block_of(q // pieces)
+        return pl.ds(pl.multiple_of(block * tokens, tokens), tokens)
+
+    def part_of(q):
+        return pl.ds(pl.multiple_of((q % pieces) * col_step, LANES), col_step)
 
     def from_root(q):
-        return cols_ref.at[span(q), pl.ds(0, width)]
+        return cols_ref.at[span(q), part_of(q)]
 
     def landed(q, which):
-        return rows_ref.at[which, span(q)]
+        return rows_ref.at[which, span(q), part_of(q)]
 
     def remote(src, q, which, send, recv, target):
         return pltpu.make_async_remote_copy(
@@ -116,48 +119,45 @@
         for i, side in enumerate(sides):
             remote(src, q, lane, side_send.at[i, q], side_recv.at[ratio - 2 - i, q], side).start()
 
-    def turn(src_ref, which, block, part):
-        at = pl.ds(pl.multiple_of(block * tokens, tokens), tokens)
-        start = pl.multiple_of(part * col_step, LANES)
-        if src_ref is cols_ref:
-            piece = src_ref[at, pl.ds(start, col_step)]
-        else:
-            piece = src_ref[which, at, pl.ds(start, col_step)]
-        out = pl.ds(pl.multiple_of(which * width + start, LANES), col_step)
-        turned_ref[out, at] = piece.T
-
-    def finish(k, part):
-        shift, block = block_of(k)
+    def turned_copy(q, which, slot):
+        start = which * width + (q % pieces) * col_step
+        at = (pl.ds(pl.multiple_of(start, LANES), col_step), span(q))
+        return pltpu.make_async_copy(turned_ref.at[at], turned_out.at[at], turned_sem.at[slot, q])
+
+    def weighted_copy(q):
+        at = (span(q), part_of(q))
+        return pltpu.make_async_copy(weighted_ref.at[at], weighted_out.at[at], weighted_sem.at[q])
+
+    def turn(piece, q, which, slot):
+        start = which * width + (q % pieces) * col_step
+        turned_ref[pl.ds(pl.multiple_of(start, LANES), col_step), span(q)] = piece.T
+        turned_copy(q, which, slot).start()
+
+    def finish(q):
+        k, part = q // pieces, q % pieces
+        shift, _ = block_of(k)
 
         @pl.when(jnp.logical_and(is_flow, jnp.logical_and(part == 0, k > 0)))
         def _():
             swapped(shift).wait_recv()
 
-        at = pl.ds(pl.multiple_of(block * tokens + part * row_step, row_step), row_step)
-        scale = cols_ref[at, pl.ds(width, LANES)].astype(jnp.float32)[:, :1]
-        weighted_ref[at, :] = (cols_ref[at, pl.ds(0, width)].astype(jnp.float32) * scale).astype(jnp.bfloat16)
-
         @pl.when(is_root)
         def _():
-            turn(cols_ref, lane, block, part)
+            turn(cols_ref[span(q), part_of(q)], q, lane, 0)
 
         @pl.when(is_flow)
         def _():
-            turn(rows_ref, lane, block, part)
+            turn(rows_ref[lane, span(q), part_of(q)], q, lane, 0)
+
+        scale = cols_ref[span(q), pl.ds(width, LANES)].astype(jnp.float32)[:, :1]
+        weighted_ref[span(q), part_of(q)] = (
+            cols_ref[span(q), part_of(q)].astype(jnp.float32) * scale).astype(jnp.bfloat16)
+        weighted_copy(q).start()
 
         for i in range(ratio - 1):
             other = lax.rem(lane + i + 1, ratio)
-
-            @pl.when(part == 0)
-            def _():
-                def arrive(j, carry):
-                    q = k * pieces + j
-                    remote(landed(q, other), q, other, side_send.at[i, q], side_recv.at[i, q], feat).wait_recv()
-                    return carry
-
-                lax.fori_loop(0, pieces, arrive, 0)
-
-            turn(rows_ref, other, block, part)
+            remote(landed(q, other), q, other, side_send.at[i, q], side_recv.at[i, q], feat).wait_recv()
+            turn(rows_ref[other, span(q), part_of(q)], q, other, 1 + i)
 
     def body(q, carry):
         k, part = q // pieces, q % pieces
@@ -176,24 +176,28 @@
             remote(landed(q, lane), q, lane, down_send.at[q], flow_recv.at[q], feat).wait_recv()
             send_on(landed(q, lane), q)
 
-        @pl.when(k > 0)
-        def _():
-            finish(k - 1, part)
+        @pl.when(q >= LAG)
+        def _():
+            finish(q - LAG)
 
         return carry
 
     lax.fori_loop(0, steps, body, 0)
 
-    def last(part, carry):
-        finish(group - 1, part)
+    def last(q, carry):
+        finish(q)
         return carry
 
-    lax.fori_loop(0, pieces, last, 0)
+    lax.fori_loop(steps - LAG, steps, last, 0)
 
     def drain(q, carry):
         here = landed(q, lane)
+        turned_copy(q, lane, 0).wait()
+        weighted_copy(q).wait()
         for i in range(ratio - 1):
+            other = lax.rem(lane + i + 1, ratio)
             remote(here, q, lane, side_send.at[i, q], side_recv.at[i, q], feat).wait_send()
+            turned_copy(q, other, 1 + i).wait()
 
         @pl.when(send_down)
         def _():
@@ -216,7 +220,7 @@
     ratio = n_feat // group
     tokens, wide = grads.shape
     width = wide + acts.shape[1]
-    pieces = next(p for p in (4, 2, 1) if width % (p * LANES) == 0)
+    pieces = next(p for p in (9, 6, 4, 3, 2, 1) if width % (p * LANES) == 0)
     steps = group * pieces
     dma = pltpu.SemaphoreType.DMA
     vmem = pl.BlockSpec(memory_space=pltpu.VMEM)
@@ -227,10 +231,13 @@
             jax.ShapeDtypeStruct((ratio * width, group * tokens), grads.dtype),
         ),
         in_specs=[vmem] * 3,
-        out_specs=(vmem, vmem),
+        out_specs=(pl.BlockSpec(memory_space=pl.ANY), pl.BlockSpec(memory_space=pl.ANY)),
         scratch_shapes=[
             pltpu.VMEM((group * tokens, width + LANES), grads.dtype),
             pltpu.VMEM((ratio, group * tokens, width), grads.dtype),
+            pltpu.VMEM((group * tokens, width), grads.dtype),
+            pltpu.VMEM((ratio * width, group * tokens), grads.dtype),
+            dma((steps,)), dma((ratio, steps)),
             dma((group,)), dma((group,)),
             dma((steps,)), dma((steps,)), dma((steps,)),
             dma((max(ratio - 1, 1), steps)), dma((max(ratio - 1, 1), steps)),
@@ -241,54 +248,61 @@
     )(grads, acts, scale)
 
 
-def gram_kernel(grad_steps, wide, inv_count, weighted_ref, turned_ref, grad_ref, act_ref):
-    step = pl.program_id(0)
-    tile = grad_ref.shape[0]
-
-    def tiles(out_ref, offset):
-        chunk = tile if out_ref.shape[1] % tile == 0 else LANES
-        for n in range(out_ref.shape[1] // chunk):
-            total = jnp.dot(turned_ref[...], weighted_ref[:, pl.ds(offset + n * chunk, chunk)],
-                            preferred_element_type=jnp.float32)
-            out_ref[:, pl.ds(n * chunk, chunk)] = (total * inv_count).astype(jnp.bfloat16)
+def gram_kernel(lane_steps, grad_steps, inv_count, weighted_ref, turned_ref, grad_ref, act_ref):
+    step = pl.program_id(0) % lane_steps
+    wide = grad_ref.shape[0]
+    tile = weighted_ref.shape[1]
+    chunk = min(tile, 256)
+
+    def fill(out_ref, start):
+        height = next(h for h in (1792, 1024, 512, 256, 128) if out_ref.shape[0] % h == 0)
+        for n in range(tile // chunk):
+            for m in range(out_ref.shape[0] // height):
+                total = jnp.dot(turned_ref[pl.ds(start + m * height, height), :],
+                                weighted_ref[:, pl.ds(n * chunk, chunk)],
+                                preferred_element_type=jnp.float32)
+                out_ref[pl.ds(m * height, height), pl.ds(n * chunk, chunk)] = (
+                    total * inv_count).astype(jnp.bfloat16)
 
     @pl.when(step < grad_steps)
     def _():
-        tiles(grad_ref, 0)
+        fill(grad_ref, 0)
 
     @pl.when(step >= grad_steps)
     def _():
-        tiles(act_ref, wide)
+        fill(act_ref, wide)
 
 
 def gram(weighted, turned, wide, narrow, inv_count):
     tokens, both = weighted.shape
     ratio = turned.shape[0] // both
     tile = next(t for t in (512, 256, 128) if wide % t == 0 and narrow % t == 0)
-    grad_tiles, act_tiles = wide // tile, narrow // tile
-    grad_steps, act_steps = ratio * grad_tiles, ratio * act_tiles
-    lane_tiles = grad_tiles + act_tiles
-
-    def row_block(i):
-        j = jnp.maximum(i - grad_steps, 0)
-        late = i >= grad_steps
-        return (jnp.where(late, (j // act_tiles) * lane_tiles + grad_tiles + j % act_tiles,
-                          (i // grad_tiles) * lane_tiles + i % grad_tiles), 0)
+    grad_steps, act_steps = wide // tile, narrow // tile
+    lane_steps = grad_steps + act_steps
+
+    def grad_block(i):
+        return i // lane_steps, jnp.minimum(i % lane_steps, grad_steps - 1)
+
+    def act_block(i):
+        lane, step = i // lane_steps, i % lane_steps
+        early = step < grad_steps
+        return (jnp.where(early, jnp.maximum(lane - 1, 0), lane),
+                jnp.where(early, jnp.where(lane > 0, act_steps - 1, 0), step - grad_steps))
 
     return pl.pallas_call(
-        functools.partial(gram_kernel, grad_steps, wide, inv_count),
-        grid=(grad_steps + act_steps,),
+        functools.partial(gram_kernel, lane_steps, grad_steps, inv_count),
+        grid=(ratio * lane_steps,),
         out_shape=(
             jax.ShapeDtypeStruct((ratio * wide, wide), jnp.bfloat16),
             jax.ShapeDtypeStruct((ratio * narrow, narrow), jnp.bfloat16),
         ),
         in_specs=[
-            pl.BlockSpec((tokens, both), lambda i: (0, 0)),
-            pl.BlockSpec((tile, tokens), row_block),
+            pl.BlockSpec((tokens, tile), lambda i: (0, i % lane_steps)),
+            pl.BlockSpec((both, tokens), lambda i: (i // lane_steps, 0)),
         ],
         out_specs=(
-            pl.BlockSpec((tile, wide), lambda i: (jnp.minimum(i, grad_steps - 1), 0)),
-            pl.BlockSpec((tile, narrow), lambda i: (jnp.maximum(i - grad_steps, 0), 0)),
+            pl.BlockSpec((wide, tile), grad_block),
+            pl.BlockSpec((narrow, tile), act_block),
         ),
         compiler_params=pltpu.CompilerParams(vmem_limit_bytes=VMEM_LIMIT),
         cost_estimate=pl.CostEstimate(

time: 165 us -> 164 us (level); the launches traced: 165 us -> 162 us
  Pallas kernels: 163 us -> 160 us
    pallas_call x1, Pallas kernels: 124 us -> 118 us  [gather_tiles(): pl.pallas_call(functools.partial(gather_kernel, sizes, pieces), out_shape...]
    pallas_call x1, Pallas kernels: 38.7 us -> 41.9 us  [gram(): pl.pallas_call(functools.partial(gram_kernel, lane_steps, grad_steps, inv...]
where the time goes in v3:
time: 164 us; the launch traced here: 162 us
  Pallas kernels  160 us (98%)
    pallas_call x1, Pallas kernels, gather_tiles(): pl.pallas_call(functools.partial(gather_kernel, sizes, pieces), out_shape...  118 us
    pallas_call x1, Pallas kernels, gram(): pl.pallas_call(functools.partial(gram_kernel, lane_steps, grad_steps, inv...  41.9 us

profile of v3, /device:TPU:5, one launch (start us, length us, event | category | flops | bytes accessed | tf_op | source)
XLA Modules:
  0.0 162.3 jit_solution(5649059264886293658)
XLA Ops:
  0.6 0.8 select_reduce_fusion
  1.4 0.7 broadcast_in_dim.23.scale_ref
  2.1 118.3 %gather_tiles.1 = (bf16[512,4608]{1,0:T(8,128)(2,1)}, bf16[9216,512]{1,0:T(8,128)(2,1)}) custom-call(bf16[128,3584]{1,0:T(8,128)(2,1)} %grads_ref.1, bf16[128,1024]{1,0:T(8,128)(2,1)} %acts_ref.1, bf16[128,128]{1,0:T(8,128)(2,1)} %broadcast_in_dim.23.scale_ref), custom_call_target="tpu_custom_call" | custom-call | tf_op jit(solution)/shard_map/gather_tiles/pallas_call | solution.py:227
  120.4 41.9 %gram.1 = (bf16[7168,3584]{1,0:T(8,128)(2,1)}, bf16[2048,1024]{1,0:T(8,128)(2,1)}) custom-call(bf16[512,4608]{1,0:T(8,128)(2,1)} %get-tuple-element.4.weighted_ref, bf16[9216,512]{1,0:T(8,128)(2,1)} %get-tuple-element.5.turned_ref), custom_call_target="tpu_custom_call" | custom-call | flops 28454158336 | bytes 69730304 | tf_op jit(solution)/shard_map/gram/pallas_call | solution.py:292
  (1 shorter events, 0.0 us)
